TPU v7x, 512 devices: a whole 4x4x16 slice. The times are simulated.
512 devices in a mesh: section: 16 (over x, y_lo, core), fsdp: 32 (over z, y_hi).
Axes of the slice: x: 4, y: 4 (y_hi: 2, y_lo: 2; y = y_hi * 2 + y_lo), z: 16, core: 2. Of those that a mesh axis runs over, the one named last changes fastest.
Arguments:
- acts: bfloat16 [16, 2, 512, 16384], P('section', None, None, 'fsdp'), may hold values from -6 to 6
- gate_up_weight: bfloat16 [16, 16384, 2048], P('section', 'fsdp'), may hold values from -0.046875 to 0.046875
- down_weight: bfloat16 [16, 1024, 16384], P('section', None, 'fsdp'), may hold values from -0.1875 to 0.1875
Outputs:
- arrived: bfloat16 [16, 2, 512, 16384], P('section', None, None, 'fsdp')
All inputs are finite; a program needn't handle non-finite values.
Results may differ from a plain program's by a relative error of at most 0.0037.
Values may be sent and summed in bfloat16 or wider, within the bound.
No kernel may reach another device: no remote copies, remote signals or barrier semaphores. Data moves between devices by JAX's collectives and lax.ppermute only.
A program may use at most 64 MiB of HBM per device.

v0:
```python
import jax
import jax.numpy as jnp
from jax import lax
from jax.sharding import PartitionSpec as P


def passed_along(block, axis, distance):
    devices = range(lax.axis_size(axis))
    route = [((i - distance) % len(devices), i) for i in devices]
    return lax.ppermute(block, axis, route)


def swiglu_rows(summed, hidden_width):
    gate_part = summed[:, :hidden_width]
    upper_part = summed[:, hidden_width:]
    return (jax.nn.silu(gate_part) * upper_part).astype(jnp.bfloat16)


def body(acts, gate_up_weight, down_weight):
    weight_in = gate_up_weight[0]
    weight_out = down_weight[0]
    hidden_width = weight_out.shape[0]
    results = []
    for micro_index in range(acts.shape[1]):
        inputs = acts[0, micro_index]
        local_terms = jnp.dot(inputs, weight_in, preferred_element_type=jnp.float32)
        summed = lax.psum(local_terms, "fsdp")
        hidden = swiglu_rows(summed, hidden_width)
        branch = jnp.dot(hidden, weight_out, preferred_element_type=jnp.float32)
        updated = (inputs.astype(jnp.float32) + branch).astype(jnp.bfloat16)
        results.append(updated)
    stacked = jnp.stack(results)[None]
    stacked = passed_along(stacked, "section", 1)
    return stacked


def solution(mesh):
    return jax.shard_map(
        body,
        mesh=mesh,
        in_specs=(
            P("section", None, None, "fsdp"),
            P("section", "fsdp", None),
            P("section", None, "fsdp"),
        ),
        out_specs=P("section", None, None, "fsdp"),
        check_vma=False,
    )
```

profile of v0, /device:TPU:6, one launch (start us, length us, event | category | flops | bytes accessed | tf_op | source)
XLA Modules:
  0.0 453.2 jit_solution(8111619341557498086)
XLA Ops:
  6.5 0.0 copy-start
  6.5 0.0 copy-start.1
  6.5 0.0 all-reduce.3.cloned.1.call-start
  6.5 1.6 copy-done
  8.1 4.3 fusion.2
  12.4 0.0 copy-done.1
  12.4 3.2 fusion.4
  15.6 0.0 all-reduce.3.cloned.1.call-update
  15.6 407.8 %all-reduce.3.cloned.1.call-done = (f32[512,2048]{1,0:T(8,128)}, f32[512,2048]{1,0:T(8,128)}) async-done(((f32[512,2048]{1,0:T(8,128)}, f32[512,2048]{1,0:T(8,128)}), (f32[512,2048]{1,0:T(8,128)}, f32[512,2048]{1,0:T(8,128)})) %all-reduce.3.cloned.1.call-update) | async-done | bytes 8388624 | tf_op jit(solution)/shard_map/psum | solution.py:27
  423.5 0.0 copy-start.2
  423.5 0.0 copy-start.3
  423.5 3.4 fusion.8
  426.8 0.4 copy-done.2
  427.2 0.3 copy-done.3
  427.5 0.7 fusion.9
  428.2 0.1 maximum_bitcast_fusion
  428.4 1.9 collective-permute-start
  430.3 15.1 %collective-permute-done = bf16[1,2,512,512]{3,2,1,0:T(8,128)(2,1)S(1)} collective-permute-done((bf16[1,2,512,512]{3,2,1,0:T(8,128)(2,1)S(1)}, bf16[1,2,512,512]{3,2,1,0:T(8,128)(2,1)S(1)}, u32[]{:S(2)}, u32[]{:S(2)}) %collective-permute-start) | collective-permute-done | bytes 1048608 | tf_op jit(solution)/shard_map/ppermute | solution.py:10
  445.4 1.0 copy.7
Async XLA Ops:
  6.5 1.6 copy-start
  6.5 5.9 %copy-start.1 = (bf16[1,2,512,512]{3,2,1,0:T(8,128)(2,1)S(1)}, bf16[1,2,512,512]{3,2,1,0:T(8,128)(2,1)}, u32[]{:S(2)}) copy-start(bf16[1,2,512,512]{3,2,1,0:T(8,128)(2,1)} %param.3) | copy-start | bytes 3145732
  6.5 416.9 %all-reduce.3.cloned.1.call-start = ((), (), s32[]{:S(2)}) async-start(), calls=%async_computation | async-start | bytes 16777216 | tf_op jit(solution)/shard_map/psum | solution.py:27
  423.5 3.8 copy-start.2
  423.5 4.1 copy-start.3
  428.4 17.0 %collective-permute-start = (bf16[1,2,512,512]{3,2,1,0:T(8,128)(2,1)S(1)}, bf16[1,2,512,512]{3,2,1,0:T(8,128)(2,1)S(1)}, u32[]{:S(2)}, u32[]{:S(2)}) collective-permute-start(bf16[1,2,512,512]{3,2,1,0:T(8,128)(2,1)S(1)} %maximum_bitcast_fusion), channel_id=1, source_target_pairs={{480,0},{0,32},{32,64},{64,96},{96,128},{128,160},{160,192},{192,2... | collective-permute-start | bytes 3145736 | tf_op jit(solution)/shard_map/ppermute | solution.py:10
Sparse Core Ops, SparseCore 0:
  15.7 407.6 all-reduce.2
where the time goes:
time: 453 us
  waiting for transfers between devices  423 us (93%)
  between operations  13.4 us (3%)
  matrix products  11.6 us (3%)
    psum x1, waiting for transfers between devices, body(): summed = lax.psum(local_terms, 'fsdp')  408 us
    ppermute x1, waiting for transfers between devices, passed_along(): return lax.ppermute(block, axis, route)  15.1 us
  transfers between devices with their start and end apart: 2, of which 2 were waited for; matrix products, arithmetic and copies ran while one was open for 0% of the time, Pallas kernels for 0%

commit v1 on v0

v1 whole, which is shorter than its diff:
```python
import jax
import jax.numpy as jnp
from jax import lax
from jax.sharding import Mesh, PartitionSpec as P

SECTIONS, RING, PAIR = 16, 16, 2


def to_next_section(block):
    return lax.ppermute(block, "section", [(i, (i + 1) % SECTIONS) for i in range(SECTIONS)])


def to_next_section_pair(block, flip):
    route = [
        (s * PAIR + y, (s + 1) % SECTIONS * PAIR + (y ^ flip))
        for s in range(SECTIONS)
        for y in range(PAIR)
    ]
    return lax.ppermute(block, ("section", "pair"), route)


def body(acts, gate_up_weight, down_weight):
    rows = acts.shape[1] * acts.shape[2]
    inputs = acts[0].reshape(rows, acts.shape[3])
    terms = jnp.dot(inputs, gate_up_weight[0], preferred_element_type=jnp.float32)
    inputs = to_next_section(inputs)
    weight_out = to_next_section(down_weight[0])
    summed = lax.psum_scatter(terms, "ring", scatter_dimension=0, tiled=True)
    summed = summed.astype(jnp.bfloat16)
    same = to_next_section_pair(summed, 0)
    other = to_next_section_pair(summed, 1)
    projected = same.astype(jnp.float32) + other.astype(jnp.float32)
    width = weight_out.shape[0]
    hidden = (jax.nn.silu(projected[:, :width]) * projected[:, width:]).astype(jnp.bfloat16)
    hidden = lax.all_gather(hidden, "ring", axis=0, tiled=True)
    branch = jnp.dot(hidden, weight_out, preferred_element_type=jnp.float32)
    updated = (inputs.astype(jnp.float32) + branch).astype(jnp.bfloat16)
    return updated.reshape(acts.shape)


def solution(mesh):
    split = Mesh(mesh.devices.reshape(SECTIONS, RING, PAIR), ("section", "ring", "pair"))
    fsdp = ("ring", "pair")
    return jax.shard_map(
        body,
        mesh=split,
        in_specs=(
            P("section", None, None, fsdp),
            P("section", fsdp, None),
            P("section", None, fsdp),
        ),
        out_specs=P("section", None, None, fsdp),
        check_vma=False,
    )
```

time: 453 us -> 224 us (0.49)
  waiting for transfers between devices: 423 us -> 183 us
  starting transfers between devices: 1.92 us -> 11.6 us
    psum x1 -> x0, waiting for transfers between devices: 408 us -> none  [body(): summed = lax.psum(local_terms, 'fsdp')]
    reduce_scatter x0 -> x1, waiting for transfers between devices: none -> 111 us  [body(): summed = lax.psum_scatter(terms, 'ring', scatter_dimension=0, tiled=True)]
    all_gather x0 -> x1, waiting for transfers between devices: none -> 40.4 us  [body(): hidden = lax.all_gather(hidden, 'ring', axis=0, tiled=True)]
    ppermute x1 -> x4, waiting for transfers between devices: 15.1 us -> 31.5 us  [the longest x2 23.5 us: to_next_section(): lax.ppermute(block, 'section', [(i, (i + 1) % SECTIONS) for i in range(SE...]
    ppermute x1 -> x4, starting transfers between devices: 1.92 us -> 11.6 us  [the longest x2 7.74 us: to_next_section_pair(): return lax.ppermute(block, ('section', 'pair'), route)]
  transfers between devices with their start and end apart: 2 -> 6, of which waited for: 2 -> 6; matrix products, arithmetic and copies ran while one was open for 0% -> 0% of each run, Pallas kernels for 0% -> 0%
where the time goes in v1:
time: 224 us; the launch traced here: 223 us
  waiting for transfers between devices  183 us (82%)
  between operations  13.5 us (6%)
  starting transfers between devices  11.6 us (5%)
  matrix products  11.2 us (5%)
  local copies, waits for them, and re-layouts  2.56 us (1%)
    reduce_scatter x1, waiting for transfers between devices, body(): summed = lax.psum_scatter(terms, 'ring', scatter_dimension=0, tiled=True)  111 us
    all_gather x1, waiting for transfers between devices, body(): hidden = lax.all_gather(hidden, 'ring', axis=0, tiled=True)  40.4 us
    ppermute x2, waiting for transfers between devices, to_next_section(): lax.ppermute(block, 'section', [(i, (i + 1) % SECTIONS) for i in range(SE...  23.5 us
    ppermute x2, waiting for transfers between devices, to_next_section_pair(): return lax.ppermute(block, ('section', 'pair'), route)  7.96 us
    ppermute x2, starting transfers between devices, to_next_section_pair(): return lax.ppermute(block, ('section', 'pair'), route)  7.74 us
    dot_general x1, matrix products, body(): jnp.dot(inputs, gate_up_weight[0], preferred_element_type=jnp.float32)  6.79 us
  transfers between devices with their start and end apart: 6, of which 6 were waited for; matrix products, arithmetic and copies ran while one was open for 0% of the time, Pallas kernels for 0%

profile of v1, /device:TPU:6, one launch (start us, length us, event | category | flops | bytes accessed | tf_op | source)
XLA Modules:
  0.0 223.2 jit_solution(16637471581793163861)
XLA Ops:
  6.5 0.0 copy-start
  6.5 0.0 reduce-scatter.2.cloned.1.call-start
  6.5 1.6 copy-done
  8.1 6.8 %fusion = f32[1024,2048]{1,0:T(8,128)} fusion(bf16[1024,512]{1,0:T(8,128)(2,1)} %bitcast.9, bf16[1,512,2048]{2,1,0:T(8,128)(2,1)S(1)} %copy-done), kind=kOutput, calls=%fused_computation | convolution fusion | flops 2147483648 | bytes 11534336 | tf_op jit(solution)/shard_map/dot_general | solution.py:25
  14.9 0.0 reduce-scatter.2.cloned.1.call-update
  14.9 0.0 copy-start.1
  15.0 0.0 all-gather.2.cloned.1.call-start
  15.0 110.6 %reduce-scatter.2.cloned.1.call-done = f32[64,2048]{1,0:T(8,128)} async-done(((f32[1024,2048]{1,0:T(8,128)}), f32[64,2048]{1,0:T(8,128)}) %reduce-scatter.2.cloned.1.call-update) | async-done | bytes 524304 | tf_op jit(solution)/shard_map/reduce_scatter | solution.py:28
  125.6 1.1 convert_element_type.19
  126.7 1.9 collective-permute-start.1
  128.6 5.8 %collective-permute-start.2 = (bf16[64,2048]{1,0:T(8,128)(2,1)S(1)}, bf16[64,2048]{1,0:T(8,128)(2,1)S(1)}, u32[]{:S(2)}, u32[]{:S(2)}) collective-permute-start(bf16[64,2048]{1,0:T(8,128)(2,1)S(1)} %convert_element_type.19), channel_id=1, source_target_pairs={{0,33},{1,32},{32,65},{33,64},{64,97},{65,96},{96,129},{97,128},{1... | collective-permute-start | bytes 786440 | tf_op jit(solution)/shard_map/ppermute | solution.py:19
  134.4 0.8 collective-permute-done.1
  135.2 7.1 %collective-permute-done.2 = bf16[64,2048]{1,0:T(8,128)(2,1)S(1)} collective-permute-done((bf16[64,2048]{1,0:T(8,128)(2,1)S(1)}, bf16[64,2048]{1,0:T(8,128)(2,1)S(1)}, u32[]{:S(2)}, u32[]{:S(2)}) %collective-permute-start.2) | collective-permute-done | bytes 262176 | tf_op jit(solution)/shard_map/ppermute | solution.py:19
  142.4 0.1 convert_add_fusion
  142.4 0.7 fusion.2
  143.2 0.0 all-gather.2.cloned.1.call-update
  143.2 0.0 copy-done.1
  143.2 1.9 collective-permute-start
  145.1 1.9 collective-permute-start.3
  147.1 13.2 %collective-permute-done = bf16[1024,512]{1,0:T(8,128)(2,1)S(1)} collective-permute-done((bf16[1024,512]{1,0:T(8,128)(2,1)S(1)}, bf16[1024,512]{1,0:T(8,128)(2,1)S(1)}, u32[]{:S(2)}, u32[]{:S(2)}) %collective-permute-start) | collective-permute-done | bytes 1048608 | tf_op jit(solution)/shard_map/ppermute | solution.py:10
  160.2 0.0 copy-start.2
  160.2 1.0 copy-done.2
  161.2 10.4 %collective-permute-done.3 = bf16[1024,512]{1,0:T(8,128)(2,1)} collective-permute-done((bf16[1024,512]{1,0:T(8,128)(2,1)}, bf16[1024,512]{1,0:T(8,128)(2,1)}, u32[]{:S(2)}, u32[]{:S(2)}) %collective-permute-start.3) | collective-permute-done | bytes 1048608 | tf_op jit(solution)/shard_map/ppermute | solution.py:10
  171.5 40.4 %all-gather.2.cloned.1.call-done = bf16[1024,1024]{1,0:T(8,128)(2,1)} async-done(((bf16[64,1024]{1,0:T(8,128)(2,1)}), bf16[1024,1024]{1,0:T(8,128)(2,1)}) %all-gather.2.cloned.1.call-update) | async-done | bytes 2097168 | tf_op jit(solution)/shard_map/all_gather | solution.py:35
  212.0 4.4 %add_convert_fusion = bf16[1024,512]{1,0:T(8,128)(2,1)} fusion(bf16[1024,512]{1,0:T(8,128)(2,1)} %copy-done.2, bf16[1024,1024]{1,0:T(8,128)(2,1)} %all-gather.2.cloned.1.call-done, bf16[1024,512]{1,0:T(8,128)(2,1)} %collective-permute-done.3), kind=kOutput, calls=%fused_computation.2 | convolution fusion | flops 1075314688 | bytes 5242880 | tf_op jit(solution)/shard_map/dot_general | solution.py:36
Async XLA Ops:
  6.5 1.6 copy-start
  6.5 119.0 %reduce-scatter.2.cloned.1.call-start = ((), (), s32[]{:S(2)}) async-start(), calls=%async_computation.1 | async-start | bytes 8912896 | tf_op jit(solution)/shard_map/reduce_scatter | solution.py:28
  14.9 128.2 %copy-start.1 = (bf16[1,2,512,512]{3,2,1,0:T(8,128)(2,1)S(1)}, bf16[1,2,512,512]{3,2,1,0:T(8,128)(2,1)}, u32[]{:S(2)}) copy-start(bf16[1,2,512,512]{3,2,1,0:T(8,128)(2,1)} %param.3) | copy-start | bytes 3145732
  15.0 197.0 %all-gather.2.cloned.1.call-start = ((), (), s32[]{:S(2)}) async-start(), calls=%async_computation.2 | async-start | bytes 2228224 | tf_op jit(solution)/shard_map/all_gather | solution.py:35
  126.7 8.6 %collective-permute-start.1 = (bf16[64,2048]{1,0:T(8,128)(2,1)S(1)}, bf16[64,2048]{1,0:T(8,128)(2,1)S(1)}, u32[]{:S(2)}, u32[]{:S(2)}) collective-permute-start(bf16[64,2048]{1,0:T(8,128)(2,1)S(1)} %convert_element_type.19), channel_id=1, source_target_pairs={{0,32},{1,33},{32,64},{33,65},{64,96},{65,97},{96,128},{97,129},{1... | collective-permute-start | bytes 786440 | tf_op jit(solution)/shard_map/ppermute | solution.py:19
  128.6 13.8 %collective-permute-start.2 = (bf16[64,2048]{1,0:T(8,128)(2,1)S(1)}, bf16[64,2048]{1,0:T(8,128)(2,1)S(1)}, u32[]{:S(2)}, u32[]{:S(2)}) collective-permute-start(bf16[64,2048]{1,0:T(8,128)(2,1)S(1)} %convert_element_type.19), channel_id=1, source_target_pairs={{0,33},{1,32},{32,65},{33,64},{64,97},{65,96},{96,129},{97,128},{1... | collective-permute-start | bytes 786440 | tf_op jit(solution)/shard_map/ppermute | solution.py:19
  143.2 17.0 %collective-permute-start = (bf16[1024,512]{1,0:T(8,128)(2,1)S(1)}, bf16[1024,512]{1,0:T(8,128)(2,1)S(1)}, u32[]{:S(2)}, u32[]{:S(2)}) collective-permute-start(bf16[1024,512]{1,0:T(8,128)(2,1)S(1)} %bitcast.10), channel_id=1, source_target_pairs={{0,32},{32,64},{64,96},{96,128},{128,160},{160,192},{192,224},{224... | collective-permute-start | bytes 3145736 | tf_op jit(solution)/shard_map/ppermute | solution.py:10
  145.1 26.4 %collective-permute-start.3 = (bf16[1024,512]{1,0:T(8,128)(2,1)}, bf16[1024,512]{1,0:T(8,128)(2,1)}, u32[]{:S(2)}, u32[]{:S(2)}) collective-permute-start(bf16[1024,512]{1,0:T(8,128)(2,1)} %bitcast.11), channel_id=1, source_target_pairs={{0,32},{32,64},{64,96},{96,128},{128,160},{160,192},{192,224},{224... | collective-permute-start | bytes 3145736 | tf_op jit(solution)/shard_map/ppermute | solution.py:10
  160.2 1.0 copy-start.2
Sparse Core Ops, SparseCore 0:
  15.1 110.4 reduce-scatter.1
  143.3 68.6 all-gather.1

commit v2 on v1

v2 whole, which is shorter than its diff:
```python
import jax
import jax.numpy as jnp
from jax import lax
from jax.sharding import Mesh, PartitionSpec as P

SECTIONS, OUTER, INNER, PAIR = 16, 4, 4, 2
BF16, F32 = jnp.bfloat16, jnp.float32


def swap_pair(block):
    return lax.ppermute(block, "pair", [(0, 1), (1, 0)])


def next_section(block, flip):
    route = [
        (s * PAIR + y, (s + 1) % SECTIONS * PAIR + (y ^ flip))
        for s in range(SECTIONS)
        for y in range(PAIR)
    ]
    return lax.ppermute(block, ("section", "pair"), route)


def inner_shift(block, distance):
    return lax.ppermute(block, "inner", [(i, (i + distance) % INNER) for i in range(INNER)])


def pick(array, index, axis):
    return lax.dynamic_index_in_dim(array, index, axis, keepdims=False)


def swiglu(projected, width):
    return (jax.nn.silu(projected[:, :width]) * projected[:, width:]).astype(BF16)


def exchange_sum(terms, axis, parts):
    got = lax.all_to_all(terms, axis, split_axis=0, concat_axis=0, tiled=True)
    got = got.reshape(parts, terms.shape[0] // parts, terms.shape[1]).astype(F32)
    return jnp.sum(got, axis=0)


def body(acts, gate_up_weight, down_weight):
    weight_in, weight_out = gate_up_weight[0], down_weight[0]
    width, columns = weight_out.shape
    batches, tokens = acts.shape[1:3]
    me, inner = lax.axis_index("pair"), lax.axis_index("inner")
    share = tokens // (PAIR * INNER * OUTER)
    halves = acts[0].reshape(batches, PAIR, tokens // PAIR, columns)

    sent = jnp.dot(pick(halves[1], 1 - me, 0), weight_in, preferred_element_type=F32).astype(BF16)
    swapped = swap_pair(sent)

    ring_rows = acts[0, 0].reshape(PAIR, INNER, OUTER, share, columns).transpose(2, 1, 0, 3, 4)
    ring_terms = jnp.dot(ring_rows.reshape(tokens, columns), weight_in, preferred_element_type=F32)
    ring_sum = lax.psum_scatter(ring_terms, ("outer", "inner"), scatter_dimension=0, tiled=True)

    kept = jnp.dot(pick(halves[1], me, 0), weight_in, preferred_element_type=F32)
    paired = (kept + swapped.astype(F32)).astype(BF16)
    run_sum = exchange_sum(paired, "inner", INNER).astype(BF16)

    mine, other = pick(halves, me, 1), pick(halves, 1 - me, 1)
    (mine, other, weight_out), run_sum = lax.optimization_barrier(((mine, other, weight_out), run_sum))
    residual_mine, residual_other = next_section(mine, 0), next_section(other, 1)
    weight_mine, weight_other = next_section(weight_out, 0), next_section(weight_out, 1)

    swap_hidden = swiglu(exchange_sum(run_sum, "outer", OUTER), width)
    swap_hidden = next_section(swap_hidden, 0)

    ring_half = ring_sum.astype(BF16).reshape(PAIR, share, 2 * width)
    ring_mine = next_section(pick(ring_half, me, 0), 0)
    ring_other = next_section(pick(ring_half, 1 - me, 0), 1)
    ring_hidden = swiglu(ring_mine.astype(F32) + ring_other.astype(F32), width)

    hidden = jnp.concatenate([ring_hidden, swap_hidden])
    hidden = lax.all_gather(hidden, "outer", axis=0, tiled=True)
    hidden = hidden.reshape(OUTER, batches, share, width).transpose(1, 0, 2, 3)
    hidden = hidden.reshape(batches * OUTER * share, width)

    weight_both = jnp.concatenate([weight_mine, weight_other], axis=1)
    residual_both = jnp.concatenate([residual_mine, residual_other], axis=2)
    residual_both = residual_both.reshape(batches, INNER, OUTER * share, 2 * columns)
    out = jnp.zeros((batches, PAIR, INNER, OUTER * share, columns), BF16)
    distances = ((0, 1), (3, 2))
    pieces = {d: inner_shift(hidden, d) if d else hidden for d in (0, 1, 3, 2)}
    for group in distances:
        updates = []
        for d in group:
            place = (inner - d) % INNER
            branch = jnp.dot(pieces[d], weight_both, preferred_element_type=F32)
            residual = pick(residual_both, place, 1).reshape(branch.shape)
            updates.append((residual.astype(F32) + branch).astype(BF16))
        foreign = swap_pair(jnp.stack([u[:, columns:] for u in updates]))
        for n, d in enumerate(group):
            place = (inner - d) % INNER
            shape = (batches, 1, 1, OUTER * share, columns)
            out = lax.dynamic_update_slice(out, updates[n][:, :columns].reshape(shape), (0, me, place, 0, 0))
            out = lax.dynamic_update_slice(out, foreign[n].reshape(shape), (0, 1 - me, place, 0, 0))
    return out.reshape(acts.shape)


def solution(mesh):
    split = Mesh(
        mesh.devices.reshape(SECTIONS, OUTER, INNER, PAIR), ("section", "outer", "inner", "pair")
    )
    fsdp = ("outer", "inner", "pair")
    return jax.shard_map(
        body,
        mesh=split,
        in_specs=(
            P("section", None, None, fsdp),
            P("section", fsdp, None),
            P("section", None, fsdp),
        ),
        out_specs=P("section", None, None, fsdp),
        check_vma=False,
    )
```

time: 224 us -> 218 us (0.973)
  the two profiles are of different devices: /device:TPU:6 before, /device:TPU:1 now
where the time goes in v2:
time: 218 us; the launch traced here: 217 us
  waiting for transfers between devices  91.7 us (42%)
  starting transfers between devices  64.3 us (29%)
  blocking collectives  22.4 us (10%)
  between operations  13.9 us (6%)
  matrix products  11.4 us (5%)
  local copies, waits for them, and re-layouts  10.1 us (5%)
  other arithmetic  3.39 us (2%)
    all_to_all x2, waiting for transfers between devices, exchange_sum(): got = lax.all_to_all(terms, axis, split_axis=0, concat_axis=0, tiled=True)  43.8 us
    ppermute x3, waiting for transfers between devices, swap_pair(): return lax.ppermute(block, 'pair', [(0, 1), (1, 0)])  28.6 us
    ppermute x7, starting transfers between devices, next_section(): return lax.ppermute(block, ('section', 'pair'), route)  24.4 us
    all_gather x1, blocking collectives, body(): hidden = lax.all_gather(hidden, 'outer', axis=0, tiled=True)  22.4 us
    all_to_all x2, starting transfers between devices, exchange_sum(): got = lax.all_to_all(terms, axis, split_axis=0, concat_axis=0, tiled=True)  20.9 us
    ppermute x3, waiting for transfers between devices, inner_shift(): lax.ppermute(block, 'inner', [(i, (i + distance) % INNER) for i in range(...  13.8 us
    ppermute x3, starting transfers between devices, swap_pair(): return lax.ppermute(block, 'pair', [(0, 1), (1, 0)])  10.1 us
    ppermute x3, starting transfers between devices, inner_shift(): lax.ppermute(block, 'inner', [(i, (i + distance) % INNER) for i in range(...  9 us
  transfers between devices with their start and end apart: 16, of which 9 were waited for; matrix products, arithmetic and copies ran while one was open for 9% of the time, Pallas kernels for 0%

profile of v2, /device:TPU:1, one launch (start us, length us, event | category | flops | bytes accessed | tf_op | source)
XLA Modules:
  0.0 217.3 jit_solution(12530016346703641005)
XLA Ops:
  6.5 1.4 fusion.21
  8.0 0.4 copy-done
  8.4 3.2 %fusion = f32[512,2048]{1,0:T(8,128)} fusion(bf16[512,512]{1,0:T(8,128)(2,1)S(1)} %bitcast.99, bf16[1,512,2048]{2,1,0:T(8,128)(2,1)S(1)} %copy-done), kind=kOutput, calls=%fused_computation.1 | convolution fusion | flops 1073741824 | bytes 6815744 | tf_op jit(solution)/shard_map/dot_general | solution.py:53
  11.7 0.0 reduce-scatter.2.cloned.1.call-update
  11.7 1.7 convolution_convert_fusion
  13.4 5.6 %collective-permute-start = (bf16[256,2048]{1,0:T(8,128)(2,1)}, bf16[256,2048]{1,0:T(8,128)(2,1)}, u32[]{:S(2)}, u32[]{:S(2)}) collective-permute-start(bf16[256,2048]{1,0:T(8,128)(2,1)} %convolution_convert_fusion), channel_id=1, source_target_pairs={{0,1},{1,0},{2,3},{3,2},{4,5},{5,4},{6,7},{7,6},{8,9},{9,8},{10,11... | collective-permute-start | bytes 3145736 | tf_op jit(solution)/shard_map/ppermute | solution.py:11
  19.1 19.9 %collective-permute-done = bf16[256,2048]{1,0:T(8,128)(2,1)} collective-permute-done((bf16[256,2048]{1,0:T(8,128)(2,1)}, bf16[256,2048]{1,0:T(8,128)(2,1)}, u32[]{:S(2)}, u32[]{:S(2)}) %collective-permute-start) | collective-permute-done | bytes 1048608 | tf_op jit(solution)/shard_map/ppermute | solution.py:11
  38.9 2.9 %add_convert_fusion = bf16[256,2048]{1,0:T(8,128)(2,1)} fusion(bf16[256,2048]{1,0:T(8,128)(2,1)} %collective-permute-done, bf16[1,512,2048]{2,1,0:T(8,128)(2,1)S(1)} %copy-done, bf16[2,256,512]{2,1,0:T(8,128)(2,1)S(1)} %bitcast.97, s32[]{:T(128)S(6)} %select_n.69), kind=kOutput, calls=%fused_computation.6 | convolution fusion | flops 538443776 | bytes 4456452 | tf_op jit(solution)/shard_map/dot_general | solution.py:56
  41.9 8.6 %all-to-all-start = ((bf16[4,64,2048]{2,1,0:T(8,128)(2,1)}), bf16[4,64,2048]{2,1,0:T(8,128)(2,1)S(1)}, u32[]{:S(2)}, u32[]{:S(2)}) async-start(bf16[4,64,2048]{2,1,0:T(8,128)(2,1)} %bitcast.8), calls=%async_computation | async-start | bytes 2097152 | tf_op jit(solution)/shard_map/all_to_all | solution.py:36
  50.5 2.3 %dynamic-slice_bitcast_fusion = (bf16[2,256,512]{2,1,0:T(8,128)(2,1)}, bf16[2,256,512]{2,1,0:T(8,128)(2,1)}) fusion(bf16[2,2,256,512]{3,2,1,0:T(8,128)(2,1)} %bitcast.95, s32[]{:T(128)S(6)} %select_n.70, s32[]{:T(128)S(6)} %select_n.69), kind=kLoop, calls=%fused_computation.17 | loop fusion | bytes 2097160 | tf_op jit(solution)/shard_map/jit(dynamic_index_in_dim)/squeeze | solution.py:28
  52.8 34.4 %all-to-all-done = bf16[4,64,2048]{2,1,0:T(8,128)(2,1)S(1)} async-done(((bf16[4,64,2048]{2,1,0:T(8,128)(2,1)}), bf16[4,64,2048]{2,1,0:T(8,128)(2,1)S(1)}, u32[]{:S(2)}, u32[]{:S(2)}) %all-to-all-start) | async-done | bytes 1048608 | tf_op jit(solution)/shard_map/all_to_all | solution.py:36
  87.2 0.9 reduce_sum.21
  88.1 6.8 %collective-permute-start.2 = (bf16[2,256,512]{2,1,0:T(8,128)(2,1)}, bf16[2,256,512]{2,1,0:T(8,128)(2,1)}, u32[]{:S(2)}, u32[]{:S(2)}) collective-permute-start(bf16[2,256,512]{2,1,0:T(8,128)(2,1)} %get-tuple-element.10), channel_id=1, source_target_pairs={{0,33},{1,32},{32,65},{33,64},{64,97},{65,96},{96,129},{97,128},{1... | collective-permute-start | bytes 1572872 | tf_op jit(solution)/shard_map/ppermute | solution.py:20
  94.9 1.9 collective-permute-start.1
  96.8 12.2 %all-to-all-start.1 = ((bf16[4,16,2048]{2,1,0:T(8,128)(2,1)}), bf16[4,16,2048]{2,1,0:T(8,128)(2,1)S(1)}, u32[]{:S(2)}, u32[]{:S(2)}) async-start(bf16[4,16,2048]{2,1,0:T(8,128)(2,1)} %bitcast.17), calls=%async_computation.2 | async-start | bytes 524288 | tf_op jit(solution)/shard_map/all_to_all | solution.py:36
  109.0 3.2 %collective-permute-start.6 = (bf16[1024,512]{1,0:T(8,128)(2,1)}, bf16[1024,512]{1,0:T(8,128)(2,1)}, u32[]{:S(2)}, u32[]{:S(2)}) collective-permute-start(bf16[1024,512]{1,0:T(8,128)(2,1)} %bitcast.118), channel_id=1, source_target_pairs={{0,32},{1,33},{32,64},{33,65},{64,96},{65,97},{96,128},{97,129},{1... | collective-permute-start | bytes 3145736 | tf_op jit(solution)/shard_map/ppermute | solution.py:20
  112.3 2.2 %collective-permute-start.7 = (bf16[1024,512]{1,0:T(8,128)(2,1)}, bf16[1024,512]{1,0:T(8,128)(2,1)S(1)}, u32[]{:S(2)}, u32[]{:S(2)}) collective-permute-start(bf16[1024,512]{1,0:T(8,128)(2,1)} %bitcast.119), channel_id=1, source_target_pairs={{0,33},{1,32},{32,65},{33,64},{64,97},{65,96},{96,129},{97,128},{1... | collective-permute-start | bytes 3145736 | tf_op jit(solution)/shard_map/ppermute | solution.py:20
  114.6 0.0 collective-permute-done.2
  114.6 0.0 collective-permute-done.1
  114.7 1.3 pad_maximum_fusion
  116.0 1.1 constant_dynamic-slice_fusion
  117.0 9.4 %all-to-all-done.1 = bf16[4,16,2048]{2,1,0:T(8,128)(2,1)S(1)} async-done(((bf16[4,16,2048]{2,1,0:T(8,128)(2,1)}), bf16[4,16,2048]{2,1,0:T(8,128)(2,1)S(1)}, u32[]{:S(2)}, u32[]{:S(2)}) %all-to-all-start.1) | async-done | bytes 262176 | tf_op jit(solution)/shard_map/all_to_all | solution.py:36
  126.5 3.4 %collective-permute-start.5 = (bf16[16,1024]{1,0:T(8,128)(2,1)S(1)}, bf16[16,1024]{1,0:T(8,128)(2,1)S(1)}, u32[]{:S(2)}, u32[]{:S(2)}) collective-permute-start(bf16[16,1024]{1,0:T(8,128)(2,1)S(1)} %fusion.17), channel_id=1, source_target_pairs={{0,32},{1,33},{32,64},{33,65},{64,96},{65,97},{96,128},{97,129},{1... | collective-permute-start | bytes 98312 | tf_op jit(solution)/shard_map/ppermute | solution.py:20
  129.9 2.0 collective-permute-done.6
  131.9 2.3 %constant_dynamic-update-slice_fusion.1 = bf16[1024,1024]{1,0:T(8,128)(2,1)} fusion(bf16[1024,512]{1,0:T(8,128)(2,1)} %collective-permute-done.6), kind=kLoop, calls=%fused_computation.38 | loop fusion | bytes 2097152
  134.2 1.0 convert_element_type.70
  135.3 4.8 %collective-permute-start.4 = (bf16[16,2048]{1,0:T(8,128)(2,1)S(1)}, bf16[16,2048]{1,0:T(8,128)(2,1)S(1)}, u32[]{:S(2)}, u32[]{:S(2)}) collective-permute-start(bf16[16,2048]{1,0:T(8,128)(2,1)S(1)} %get-tuple-element.34), channel_id=1, source_target_pairs={{0,33},{1,32},{32,65},{33,64},{64,97},{65,96},{96,129},{97,128},{1... | collective-permute-start | bytes 196616 | tf_op jit(solution)/shard_map/ppermute | solution.py:20
  140.1 1.9 collective-permute-start.3
  142.0 3.4 %collective-permute-done.7 = bf16[1024,512]{1,0:T(8,128)(2,1)S(1)} collective-permute-done((bf16[1024,512]{1,0:T(8,128)(2,1)}, bf16[1024,512]{1,0:T(8,128)(2,1)S(1)}, u32[]{:S(2)}, u32[]{:S(2)}) %collective-permute-start.7) | collective-permute-done | bytes 1048608 | tf_op jit(solution)/shard_map/ppermute | solution.py:20
  145.4 1.1 constant_dynamic-update-slice_fusion
  146.6 0.2 collective-permute-done.4
  146.8 0.0 collective-permute-done.3
  146.9 22.4 %all_gather.3 = bf16[128,1024]{1,0:T(8,128)(2,1)S(1)} all-gather(bf16[32,1024]{1,0:T(8,128)(2,1)S(1)} %pad_maximum_fusion.3), channel_id=1, replica_groups=mesh['section'=16,'outer'=4,'inner'=4,'pair'=2] {'outer'}, dimensions={0}, use_global_device_ids=true | all-gather | bytes 327680 | tf_op jit(solution)/shard_map/all_gather | solution.py:74
  169.3 1.9 collective-permute-start.8
  171.2 5.2 %collective-permute-start.10 = (bf16[128,1024]{1,0:T(8,128)(2,1)S(1)}, bf16[128,1024]{1,0:T(8,128)(2,1)S(1)}, u32[]{:S(2)}, u32[]{:S(2)}) collective-permute-start(bf16[128,1024]{1,0:T(8,128)(2,1)S(1)} %bitcast.106), channel_id=1, source_target_pairs={{0,6},{2,0},{4,2},{6,4},{1,7},{3,1},{5,3},{7,5},{8,14},{10,8},{12,... | collective-permute-start | bytes 786440 | tf_op jit(solution)/shard_map/ppermute | solution.py:24
  176.4 1.9 collective-permute-start.11
  178.4 2.2 %fusion.5 = bf16[128,1024]{1,0:T(8,128)(2,1)S(1)} fusion(bf16[128,1024]{1,0:T(8,128)(2,1)S(1)} %bitcast.108, bf16[1024,1024]{1,0:T(8,128)(2,1)} %constant_dynamic-update-slice_fusion, bf16[128,1024]{1,0:T(8,128)(2,1)S(1)} %bitcast.104), kind=kOutput, calls=%fused_computation.11 | convolution fusion | flops 268828672 | bytes 2883584 | tf_op jit(solution)/shard_map/dot_general | solution.py:88
  180.6 0.1 broadcast_in_dim.3
  180.8 0.4 fusion.6
  181.3 2.6 %collective-permute-start.9 = (bf16[2,128,512]{2,1,0:T(8,128)(2,1)S(1)}, bf16[2,128,512]{2,1,0:T(8,128)(2,1)S(1)}, u32[]{:S(2)}, u32[]{:S(2)}) collective-permute-start(bf16[2,128,512]{2,1,0:T(8,128)(2,1)S(1)} %pad_maximum_fusion.1), channel_id=1, source_target_pairs={{0,1},{1,0},{2,3},{3,2},{4,5},{5,4},{6,7},{7,6},{8,9},{9,8},{10,11... | collective-permute-start | bytes 786440 | tf_op jit(solution)/shard_map/ppermute | solution.py:11
  183.8 2.9 %collective-permute-done.10 = bf16[128,1024]{1,0:T(8,128)(2,1)S(1)} collective-permute-done((bf16[128,1024]{1,0:T(8,128)(2,1)S(1)}, bf16[128,1024]{1,0:T(8,128)(2,1)S(1)}, u32[]{:S(2)}, u32[]{:S(2)}) %collective-permute-start.10) | collective-permute-done | bytes 262176 | tf_op jit(solution)/shard_map/ppermute | solution.py:24
  186.8 0.4 fusion.7
  187.3 10.8 %collective-permute-done.11 = bf16[128,1024]{1,0:T(8,128)(2,1)S(1)} collective-permute-done((bf16[128,1024]{1,0:T(8,128)(2,1)S(1)}, bf16[128,1024]{1,0:T(8,128)(2,1)S(1)}, u32[]{:S(2)}, u32[]{:S(2)}) %collective-permute-start.11) | collective-permute-done | bytes 262176 | tf_op jit(solution)/shard_map/ppermute | solution.py:24
  198.1 0.4 fusion.8
  198.6 1.9 collective-permute-start.12
  200.7 8.7 %collective-permute-done.12 = bf16[2,128,512]{2,1,0:T(8,128)(2,1)S(1)} collective-permute-done((bf16[2,128,512]{2,1,0:T(8,128)(2,1)S(1)}, bf16[2,128,512]{2,1,0:T(8,128)(2,1)S(1)}, u32[]{:S(2)}, u32[]{:S(2)}) %collective-permute-start.12) | collective-permute-done | bytes 262176 | tf_op jit(solution)/shard_map/ppermute | solution.py:11
  209.5 0.0 copy-start.2
  209.5 1.0 copy-done.2
  (40 shorter events, 0.5 us)
Async XLA Ops:
  6.5 1.9 copy-start
  6.5 127.7 %reduce-scatter.2.cloned.1.call-start = ((), (), s32[]{:S(2)}) async-start(), calls=%async_computation.3 | async-start | bytes 4456448 | tf_op jit(solution)/shard_map/reduce_scatter | solution.py:54
  13.4 25.5 %collective-permute-start = (bf16[256,2048]{1,0:T(8,128)(2,1)}, bf16[256,2048]{1,0:T(8,128)(2,1)}, u32[]{:S(2)}, u32[]{:S(2)}) collective-permute-start(bf16[256,2048]{1,0:T(8,128)(2,1)} %convolution_convert_fusion), channel_id=1, source_target_pairs={{0,1},{1,0},{2,3},{3,2},{4,5},{5,4},{6,7},{7,6},{8,9},{9,8},{10,11... | collective-permute-start | bytes 3145736 | tf_op jit(solution)/shard_map/ppermute | solution.py:11
  41.9 45.4 %all-to-all-start = ((bf16[4,64,2048]{2,1,0:T(8,128)(2,1)}), bf16[4,64,2048]{2,1,0:T(8,128)(2,1)S(1)}, u32[]{:S(2)}, u32[]{:S(2)}) async-start(bf16[4,64,2048]{2,1,0:T(8,128)(2,1)} %bitcast.8), calls=%async_computation | async-start | bytes 2097152 | tf_op jit(solution)/shard_map/all_to_all | solution.py:36
  88.1 26.5 %collective-permute-start.2 = (bf16[2,256,512]{2,1,0:T(8,128)(2,1)}, bf16[2,256,512]{2,1,0:T(8,128)(2,1)}, u32[]{:S(2)}, u32[]{:S(2)}) collective-permute-start(bf16[2,256,512]{2,1,0:T(8,128)(2,1)} %get-tuple-element.10), channel_id=1, source_target_pairs={{0,33},{1,32},{32,65},{33,64},{64,97},{65,96},{96,129},{97,128},{1... | collective-permute-start | bytes 1572872 | tf_op jit(solution)/shard_map/ppermute | solution.py:20
  94.9 19.7 %collective-permute-start.1 = (bf16[2,256,512]{2,1,0:T(8,128)(2,1)}, bf16[2,256,512]{2,1,0:T(8,128)(2,1)}, u32[]{:S(2)}, u32[]{:S(2)}) collective-permute-start(bf16[2,256,512]{2,1,0:T(8,128)(2,1)} %get-tuple-element.9), channel_id=1, source_target_pairs={{0,32},{1,33},{32,64},{33,65},{64,96},{65,97},{96,128},{97,129},{1... | collective-permute-start | bytes 1572872 | tf_op jit(solution)/shard_map/ppermute | solution.py:20
  96.8 29.6 %all-to-all-start.1 = ((bf16[4,16,2048]{2,1,0:T(8,128)(2,1)}), bf16[4,16,2048]{2,1,0:T(8,128)(2,1)S(1)}, u32[]{:S(2)}, u32[]{:S(2)}) async-start(bf16[4,16,2048]{2,1,0:T(8,128)(2,1)} %bitcast.17), calls=%async_computation.2 | async-start | bytes 524288 | tf_op jit(solution)/shard_map/all_to_all | solution.py:36
  109.0 22.9 %collective-permute-start.6 = (bf16[1024,512]{1,0:T(8,128)(2,1)}, bf16[1024,512]{1,0:T(8,128)(2,1)}, u32[]{:S(2)}, u32[]{:S(2)}) collective-permute-start(bf16[1024,512]{1,0:T(8,128)(2,1)} %bitcast.118), channel_id=1, source_target_pairs={{0,32},{1,33},{32,64},{33,65},{64,96},{65,97},{96,128},{97,129},{1... | collective-permute-start | bytes 3145736 | tf_op jit(solution)/shard_map/ppermute | solution.py:20
  112.3 33.1 %collective-permute-start.7 = (bf16[1024,512]{1,0:T(8,128)(2,1)}, bf16[1024,512]{1,0:T(8,128)(2,1)S(1)}, u32[]{:S(2)}, u32[]{:S(2)}) collective-permute-start(bf16[1024,512]{1,0:T(8,128)(2,1)} %bitcast.119), channel_id=1, source_target_pairs={{0,33},{1,32},{32,65},{33,64},{64,97},{65,96},{96,129},{97,128},{1... | collective-permute-start | bytes 3145736 | tf_op jit(solution)/shard_map/ppermute | solution.py:20
  126.5 20.4 %collective-permute-start.5 = (bf16[16,1024]{1,0:T(8,128)(2,1)S(1)}, bf16[16,1024]{1,0:T(8,128)(2,1)S(1)}, u32[]{:S(2)}, u32[]{:S(2)}) collective-permute-start(bf16[16,1024]{1,0:T(8,128)(2,1)S(1)} %fusion.17), channel_id=1, source_target_pairs={{0,32},{1,33},{32,64},{33,65},{64,96},{65,97},{96,128},{97,129},{1... | collective-permute-start | bytes 98312 | tf_op jit(solution)/shard_map/ppermute | solution.py:20
  134.2 44.1 %copy-start.6 = (bf16[2,1,64,1024]{3,2,1,0:T(8,128)(2,1)S(1)}, bf16[2,1,64,1024]{3,2,1,0:T(8,128)(2,1)}, u32[]{:S(2)}) copy-start(bf16[2,1,64,1024]{3,2,1,0:T(8,128)(2,1)} %get-tuple-element.16) | copy-start | bytes 786436
  135.3 11.5 %collective-permute-start.4 = (bf16[16,2048]{1,0:T(8,128)(2,1)S(1)}, bf16[16,2048]{1,0:T(8,128)(2,1)S(1)}, u32[]{:S(2)}, u32[]{:S(2)}) collective-permute-start(bf16[16,2048]{1,0:T(8,128)(2,1)S(1)} %get-tuple-element.34), channel_id=1, source_target_pairs={{0,33},{1,32},{32,65},{33,64},{64,97},{65,96},{96,129},{97,128},{1... | collective-permute-start | bytes 196616 | tf_op jit(solution)/shard_map/ppermute | solution.py:20
  140.1 6.7 %collective-permute-start.3 = (bf16[16,2048]{1,0:T(8,128)(2,1)S(1)}, bf16[16,2048]{1,0:T(8,128)(2,1)S(1)}, u32[]{:S(2)}, u32[]{:S(2)}) collective-permute-start(bf16[16,2048]{1,0:T(8,128)(2,1)S(1)} %get-tuple-element.33), channel_id=1, source_target_pairs={{0,32},{1,33},{32,64},{33,65},{64,96},{65,97},{96,128},{97,129},{1... | collective-permute-start | bytes 196616 | tf_op jit(solution)/shard_map/ppermute | solution.py:20
  169.3 11.4 %collective-permute-start.8 = (bf16[128,1024]{1,0:T(8,128)(2,1)S(1)}, bf16[128,1024]{1,0:T(8,128)(2,1)S(1)}, u32[]{:S(2)}, u32[]{:S(2)}) collective-permute-start(bf16[128,1024]{1,0:T(8,128)(2,1)S(1)} %bitcast.105), channel_id=1, source_target_pairs={{0,2},{2,4},{4,6},{6,0},{1,3},{3,5},{5,7},{7,1},{8,10},{10,12},{12... | collective-permute-start | bytes 786440 | tf_op jit(solution)/shard_map/ppermute | solution.py:24
  171.2 15.6 %collective-permute-start.10 = (bf16[128,1024]{1,0:T(8,128)(2,1)S(1)}, bf16[128,1024]{1,0:T(8,128)(2,1)S(1)}, u32[]{:S(2)}, u32[]{:S(2)}) collective-permute-start(bf16[128,1024]{1,0:T(8,128)(2,1)S(1)} %bitcast.106), channel_id=1, source_target_pairs={{0,6},{2,0},{4,2},{6,4},{1,7},{3,1},{5,3},{7,5},{8,14},{10,8},{12,... | collective-permute-start | bytes 786440 | tf_op jit(solution)/shard_map/ppermute | solution.py:24
  176.4 21.7 %collective-permute-start.11 = (bf16[128,1024]{1,0:T(8,128)(2,1)S(1)}, bf16[128,1024]{1,0:T(8,128)(2,1)S(1)}, u32[]{:S(2)}, u32[]{:S(2)}) collective-permute-start(bf16[128,1024]{1,0:T(8,128)(2,1)S(1)} %bitcast.107), channel_id=1, source_target_pairs={{0,4},{2,6},{4,0},{6,2},{1,5},{3,7},{5,1},{7,3},{8,12},{10,14},{12... | collective-permute-start | bytes 786440 | tf_op jit(solution)/shard_map/ppermute | solution.py:24
  178.3 2.4 %copy-start.1 = (bf16[1024,1024]{1,0:T(8,128)(2,1)S(1)}, bf16[1024,1024]{1,0:T(8,128)(2,1)}, u32[]{:S(2)}) copy-start(bf16[1024,1024]{1,0:T(8,128)(2,1)} %constant_dynamic-update-slice_fusion) | copy-start | bytes 6291460
  178.4 2.4 %copy-start.5 = (bf16[2,1,64,1024]{3,2,1,0:T(8,128)(2,1)S(1)}, bf16[2,1,64,1024]{3,2,1,0:T(8,128)(2,1)}, u32[]{:S(2)}) copy-start(bf16[2,1,64,1024]{3,2,1,0:T(8,128)(2,1)} %get-tuple-element.15) | copy-start | bytes 786436
  180.7 6.1 %copy-start.4 = (bf16[2,1,64,1024]{3,2,1,0:T(8,128)(2,1)S(1)}, bf16[2,1,64,1024]{3,2,1,0:T(8,128)(2,1)}, u32[]{:S(2)}) copy-start(bf16[2,1,64,1024]{3,2,1,0:T(8,128)(2,1)} %get-tuple-element.14) | copy-start | bytes 786436
  181.2 16.8 %copy-start.3 = (bf16[2,1,64,1024]{3,2,1,0:T(8,128)(2,1)S(1)}, bf16[2,1,64,1024]{3,2,1,0:T(8,128)(2,1)}, u32[]{:S(2)}) copy-start(bf16[2,1,64,1024]{3,2,1,0:T(8,128)(2,1)} %get-tuple-element.13) | copy-start | bytes 786436
  181.3 19.2 %collective-permute-start.9 = (bf16[2,128,512]{2,1,0:T(8,128)(2,1)S(1)}, bf16[2,128,512]{2,1,0:T(8,128)(2,1)S(1)}, u32[]{:S(2)}, u32[]{:S(2)}) collective-permute-start(bf16[2,128,512]{2,1,0:T(8,128)(2,1)S(1)} %pad_maximum_fusion.1), channel_id=1, source_target_pairs={{0,1},{1,0},{2,3},{3,2},{4,5},{5,4},{6,7},{7,6},{8,9},{9,8},{10,11... | collective-permute-start | bytes 786440 | tf_op jit(solution)/shard_map/ppermute | solution.py:11
  198.6 10.8 %collective-permute-start.12 = (bf16[2,128,512]{2,1,0:T(8,128)(2,1)S(1)}, bf16[2,128,512]{2,1,0:T(8,128)(2,1)S(1)}, u32[]{:S(2)}, u32[]{:S(2)}) collective-permute-start(bf16[2,128,512]{2,1,0:T(8,128)(2,1)S(1)} %pad_maximum_fusion.2), channel_id=1, source_target_pairs={{0,1},{1,0},{2,3},{3,2},{4,5},{5,4},{6,7},{7,6},{8,9},{9,8},{10,11... | collective-permute-start | bytes 786440 | tf_op jit(solution)/shard_map/ppermute | solution.py:11
  209.5 1.0 copy-start.2
Sparse Core Ops, SparseCore 0:
  11.8 96.1 reduce-scatter.1
